TPU v7x, 256 devices: a whole 4x4x8 slice. The times are simulated.
256 devices in a mesh: gx: 8 (over x, core), gy: 32 (over y, z).
Axes of the slice: x: 4, y: 4, z: 8, core: 2. Of those that a mesh axis runs over, the one named last changes fastest.
Arguments:
- tokens: bfloat16 [512, 16384], P(None, ('gx', 'gy')), may hold values from -6 to 6
- gate_weight: bfloat16 [16384, 32768], P('gx', 'gy'), may hold values from -0.046875 to 0.046875
- up_weight: bfloat16 [16384, 32768], P('gx', 'gy'), may hold values from -0.046875 to 0.046875
- down_weight: bfloat16 [32, 1024, 16384], P(None, 'gx', 'gy'), may hold values from -0.03125 to 0.03125
Outputs:
- mixed: bfloat16 [512, 16384], P('gx', 'gy')
All inputs are finite; a program needn't handle non-finite values.
Results may differ from a plain program's by a relative error of at most 0.005.
Values may be sent and summed in bfloat16 or wider, within the bound.
A program may use at most 64 MiB of HBM per device.

v0:
```python
import jax
import jax.numpy as jnp
from jax import lax
from jax.sharding import PartitionSpec as P


def body(tokens, gate_weight, up_weight, down_weight):
    columns = gate_weight.shape[1]
    piece = lax.all_gather(tokens, "gy", axis=1, tiled=True)
    gate = jnp.dot(piece, gate_weight, preferred_element_type=jnp.float32)
    up = jnp.dot(piece, up_weight, preferred_element_type=jnp.float32)
    gate_full, up_full = lax.psum((gate, up), "gx")
    width = columns // lax.axis_size("gx")
    offset = lax.axis_index("gx") * width
    gate_share = lax.dynamic_slice_in_dim(gate_full, offset, width, 1)
    up_share = lax.dynamic_slice_in_dim(up_full, offset, width, 1)
    hidden = (jax.nn.silu(gate_share) * up_share).astype(jnp.bfloat16)
    down_flat = down_weight.reshape(-1, down_weight.shape[2])
    partial_out = jnp.dot(
        lax.all_gather(hidden, "gy", axis=1, tiled=True),
        down_flat,
        preferred_element_type=jnp.float32,
    )
    mixed = lax.psum_scatter(partial_out, "gx", scatter_dimension=0, tiled=True)
    return mixed.astype(jnp.bfloat16)


def solution(mesh):
    in_specs = (P(None, ("gx", "gy")), P("gx", "gy"), P("gx", "gy"), P(None, "gx", "gy"))
    out_specs = P("gx", "gy")
    return jax.shard_map(body, mesh=mesh, in_specs=in_specs, out_specs=out_specs, check_vma=False)
```

profile of v0, /device:TPU:1, one launch (start us, length us, event | category | flops | bytes accessed | tf_op | source)
XLA Modules:
  0.0 310.2 jit_solution(15390831393990860293)
XLA Ops:
  6.5 0.0 all-gather.3.cloned.1.call-start
  6.5 0.7 all-gather.3.cloned.1.call-update
  7.3 0.0 all-reduce.3.cloned.1.call-start
  7.3 80.5 %all-gather.3.cloned.1.call-done = bf16[512,2048]{0,1:T(8,128)(2,1)} async-done(((bf16[512,64]{0,1:T(8,128)(2,1)}), bf16[512,2048]{0,1:T(8,128)(2,1)}) %all-gather.3.cloned.1.call-update) | async-done | bytes 2097168 | tf_op jit(solution)/shard_map/all_gather | solution.py:9
  87.8 0.0 copy-start
  87.8 0.0 copy-start.1
  87.8 6.6 %fusion.1 = f32[512,1024]{1,0:T(8,128)} fusion(bf16[512,2048]{0,1:T(8,128)(2,1)} %all-gather.3.cloned.1.call-done, bf16[2048,1024]{1,0:T(8,128)(2,1)} %param.6), kind=kOutput, calls=%fused_computation.2 | convolution fusion | flops 2147483648 | bytes 8388608 | tf_op jit(solution)/shard_map/dot_general | solution.py:11
  94.5 0.0 copy-done
  94.5 0.0 copy-done.1
  94.5 3.7 %fusion = f32[512,1024]{1,0:T(8,128)} fusion(bf16[512,2048]{0,1:T(8,128)(2,1)S(1)} %copy-done.1, bf16[2048,1024]{1,0:T(8,128)(2,1)S(1)} %copy-done), kind=kOutput, calls=%fused_computation.1 | convolution fusion | flops 2147483648 | bytes 8388608 | tf_op jit(solution)/shard_map/dot_general | solution.py:10
  98.2 0.0 all-reduce.3.cloned.1.call-update
  98.2 0.0 all-gather.5.cloned.1.call-start
  98.3 77.3 %all-reduce.3.cloned.1.call-done = (f32[512,1024]{1,0:T(8,128)}, f32[512,1024]{1,0:T(8,128)}) async-done(((f32[512,1024]{1,0:T(8,128)}, f32[512,1024]{1,0:T(8,128)}), (f32[512,1024]{1,0:T(8,128)}, f32[512,1024]{1,0:T(8,128)})) %all-reduce.3.cloned.1.call-update) | async-done | bytes 4194320 | tf_op jit(solution)/shard_map/psum | solution.py:12
  175.5 1.8 multiply_convert_fusion
  177.3 0.0 all-gather.5.cloned.1.call-update
  177.3 0.0 reduce-scatter.2.cloned.1.call-start
  177.4 82.5 %all-gather.5.cloned.1.call-done = bf16[512,4096]{1,0:T(8,128)(2,1)} async-done(((bf16[512,128]{1,0:T(8,128)(2,1)}), bf16[512,4096]{1,0:T(8,128)(2,1)}) %all-gather.5.cloned.1.call-update) | async-done | bytes 4194320 | tf_op jit(solution)/shard_map/all_gather | solution.py:20
  259.9 6.8 %fusion.2 = f32[512,512]{1,0:T(8,128)} fusion(bf16[512,4096]{1,0:T(8,128)(2,1)} %all-gather.5.cloned.1.call-done, bf16[4096,512]{1,0:T(8,128)(2,1)} %bitcast.7), kind=kOutput, calls=%fused_computation.3 | convolution fusion | flops 2147483648 | bytes 9437184 | tf_op jit(solution)/shard_map/dot_general | solution.py:19
  266.6 0.0 reduce-scatter.2.cloned.1.call-update
  266.7 35.5 %reduce-scatter.2.cloned.1.call-done = f32[64,512]{1,0:T(8,128)} async-done(((f32[512,512]{1,0:T(8,128)}), f32[64,512]{1,0:T(8,128)}) %reduce-scatter.2.cloned.1.call-update) | async-done | bytes 131088 | tf_op jit(solution)/shard_map/reduce_scatter | solution.py:24
  302.1 1.5 convert_element_type.7
Async XLA Ops:
  6.5 81.3 %all-gather.3.cloned.1.call-start = ((), (), s32[]{:S(2)}) async-start(), calls=%async_computation.1 | async-start | bytes 2162688 | tf_op jit(solution)/shard_map/all_gather | solution.py:9
  7.3 168.3 %all-reduce.3.cloned.1.call-start = ((), (), s32[]{:S(2)}) async-start(), calls=%async_computation.4 | async-start | bytes 8388608 | tf_op jit(solution)/shard_map/psum | solution.py:12
  87.8 6.7 %copy-start = (bf16[2048,1024]{1,0:T(8,128)(2,1)S(1)}, bf16[2048,1024]{1,0:T(8,128)(2,1)}, u32[]{:S(2)}) copy-start(bf16[2048,1024]{1,0:T(8,128)(2,1)} %param.5) | copy-start | bytes 12582916
  87.8 6.7 %copy-start.1 = (bf16[512,2048]{0,1:T(8,128)(2,1)S(1)}, bf16[512,2048]{0,1:T(8,128)(2,1)}, u32[]{:S(2)}) copy-start(bf16[512,2048]{0,1:T(8,128)(2,1)} %all-gather.3.cloned.1.call-done) | copy-start | bytes 6291460
  98.2 161.7 %all-gather.5.cloned.1.call-start = ((), (), s32[]{:S(2)}) async-start(), calls=%async_computation.2 | async-start | bytes 4325376 | tf_op jit(solution)/shard_map/all_gather | solution.py:20
  177.3 124.8 %reduce-scatter.2.cloned.1.call-start = ((), (), s32[]{:S(2)}) async-start(), calls=%async_computation.3 | async-start | bytes 1179648 | tf_op jit(solution)/shard_map/reduce_scatter | solution.py:24
Sparse Core Ops, SparseCore 0:
  9.9 77.8 all-gather.2
  98.3 77.1 all-reduce.2
  178.0 81.8 all-gather.4
  266.8 35.3 reduce-scatter.1
where the time goes:
time: 312 us; the launch traced here: 310 us
  waiting for transfers between devices  277 us (89%)
  matrix products  17.1 us (5%)
  between operations  13.1 us (4%)
  other arithmetic  3.29 us (1%)
    all_gather x1, waiting for transfers between devices, body(): lax.all_gather(hidden, 'gy', axis=1, tiled=True)  82.5 us
    all_gather x1, waiting for transfers between devices, body(): piece = lax.all_gather(tokens, 'gy', axis=1, tiled=True)  80.5 us
    psum x1, waiting for transfers between devices, body(): gate_full, up_full = lax.psum((gate, up), 'gx')  77.3 us
    reduce_scatter x1, waiting for transfers between devices, body(): mixed = lax.psum_scatter(partial_out, 'gx', scatter_dimension=0, tiled=True)  35.5 us
    dot_general x1, matrix products, body(): jnp.dot(lax.all_gather(hidden, 'gy', axis=1, tiled=True), down_flat, pref...  6.75 us
    dot_general x1, matrix products, body(): up = jnp.dot(piece, up_weight, preferred_element_type=jnp.float32)  6.64 us
  transfers between devices with their start and end apart: 4, of which 4 were waited for; matrix products, arithmetic and copies ran while one was open for 0% of the time, Pallas kernels for 0%

commit v1 on v0

v1 whole, which is shorter than its diff:
```python
import functools

import jax
import jax.numpy as jnp
from jax import lax
from jax.experimental import pallas as pl
from jax.experimental.pallas import tpu as pltpu
from jax.sharding import PartitionSpec as P

MESH = pl.DeviceIdType.MESH
NX, NC, NY, NZ = 4, 2, 4, 8
CHUNKS = 4
ROWS = 128
HALF = ROWS // 2
PK = HALF // 2
SEMS = 320

RING4 = [[(0, 1, None), (0, -1, None)], [(-1, 1, 0), (1, -1, 1)]]
RING8 = [
    [(0, 1, None), (0, -1, None)],
    [(-1, 1, None), (1, -1, None)],
    [(-2, 1, None), (2, -1, None)],
    [(-3, 1, 0), (3, -1, 1)],
]
FAST4 = [[(0, 2, None), (0, 1, None), (0, -1, None)]]
FAST8 = [
    [(0, 2, None), (0, -2, None), (0, 1, None), (0, -1, None)],
    [(-2, 2, 0), (2, -2, 1), (-2, 1, None), (2, -1, None)],
]


def kernel(
    tok_hbm, gate_hbm, up_hbm, down_hbm, out_ref,
    tok, w1, wd, tok_p, tok_q, lhs, own, part_out, part_in, sum_out, sum_in,
    hid_p, hid_q, acc, acc_in, red_out, red_in,
    load_sem, send_sem, recv_sem,
):
    gx, gy = lax.axis_index("gx"), lax.axis_index("gy")
    x, core, y, z = gx // NC, gx % NC, gy // NZ, gy % NZ

    def at(dx=0, dc=0, dy=0, dz=0):
        return (
            (x + dx + NX) % NX * NC + (core + dc) % NC,
            (y + dy + NY) % NY * NZ + (z + dz + NZ) % NZ,
        )

    started = []

    def send(src, dst, device):
        k = len(started)
        copy = pltpu.make_async_remote_copy(
            src_ref=src, dst_ref=dst, send_sem=send_sem.at[k], recv_sem=recv_sem.at[k],
            device_id=device, device_id_type=MESH,
        )
        copy.start()
        started.append(copy)
        return copy

    load = pltpu.make_async_copy(tok_hbm, tok, load_sem.at[0])
    load.start()
    w_loads = []
    for slot in range(8):
        dc, dx = (1 - slot // 4), slot % 4
        share = (x + dx) % NX * NC + (core + dc) % NC
        columns = pl.ds(pl.multiple_of(share * 128, 128), 128)
        for h, src in enumerate((gate_hbm, up_hbm)):
            copy = pltpu.make_async_copy(
                src.at[:, columns], w1.at[slot, :, pl.ds(h * 128, 128)], load_sem.at[2 + 2 * slot + h]
            )
            copy.start()
            w_loads.append(copy)
    wd_load = pltpu.make_async_copy(down_hbm, wd, load_sem.at[1])
    wd_load.start()

    barrier = pltpu.get_barrier_semaphore()
    peers = [at(dy=d) for d in (1, -1, 2)] + [at(dz=d) for d in (1, -1, 2, -2)]
    peers += [at(dx=d) for d in (1, 2, 3)] + [at(dc=1)]
    for peer in peers:
        pl.semaphore_signal(barrier, inc=1, device_id=peer, device_id_type=MESH)

    load.wait()
    for ch in range(CHUNKS):
        side = []
        for c in range(NC):
            side.append(jnp.concatenate(
                [tok[(i * NC + c) * 64 + ch * 16:(i * NC + c) * 64 + ch * 16 + 16, :] for i in range(NX)], axis=0
            ))
        packed = jnp.concatenate(side, axis=1)
        tok_p[ch, z, y] = packed[:PK]
        tok_q[ch, y, z] = packed[PK:]
    pl.semaphore_wait(barrier, len(peers))

    def halved(ref, lead, half, size):
        if half is None:
            return ref.at[lead]
        return ref.at[lead + (pl.ds(half * size // 2, size // 2),)]

    class Gather:
        def __init__(self, ref, ch, first, plans, rows):
            self.ref, self.ch, self.first, self.rows = ref, ch, first, rows
            self.steps = [(0, s) for s in plans[0]] + [(1, s) for s in plans[1]]
            self.next = 0
            self.flying = []

        def start(self):
            phase, step = self.steps[self.next]
            self.next += 1
            along_y = (phase == 0) == (self.first == "y")
            n, me = (NY, y) if along_y else (NZ, z)
            for source, shift, half in step:
                block = (me + source + n) % n
                if phase == 0:
                    lead = (self.ch, z, block) if along_y else (self.ch, y, block)
                    part = halved(self.ref, lead, half, self.rows)
                else:
                    size = NZ if along_y else NY
                    part = halved(self.ref, (self.ch, block), half, size)
                device = at(dy=shift) if along_y else at(dz=shift)
                self.flying.append(send(part, part, device))

        def wait(self):
            for copy in self.flying:
                copy.wait_recv()
            self.flying = []

        def advance(self):
            self.wait()
            if self.next < len(self.steps):
                self.start()

    tok_plans = (FAST4, FAST8)
    gp = [Gather(tok_p, ch, "y", (tok_plans[0], tok_plans[1]), PK) for ch in range(CHUNKS)]
    gq = [Gather(tok_q, ch, "z", (tok_plans[1], tok_plans[0]), PK) for ch in range(CHUNKS)]
    hp = [Gather(hid_p, ch, "y", (RING4, RING8), HALF) for ch in range(CHUNKS)]
    hq = [Gather(hid_q, ch, "z", (RING8, RING4), HALF) for ch in range(CHUNKS)]

    summing = [[] for _ in range(CHUNKS)]

    def project(ch):
        gp[ch].wait()
        gq[ch].wait()
        for b in range(NY):
            for a in range(0, NZ, 2):
                for first, ref in ((0, tok_p.at[ch, a:a + 2, b]), (PK, tok_q.at[ch, b, a:a + 2])):
                    lo, hi = ref[0], ref[1]
                    columns = slice((b * NZ + a) * 64, (b * NZ + a) * 64 + 128)
                    lhs[first:first + PK, columns] = jnp.concatenate([lo[:, :64], hi[:, :64]], axis=1)
                    lhs[HALF + first:HALF + first + PK, columns] = jnp.concatenate([lo[:, 64:], hi[:, 64:]], axis=1)
        partner = [None] * 4
        for i in (2, 1, 3, 0):
            if ch == 0:
                w_loads[2 * i].wait()
                w_loads[2 * i + 1].wait()
            part_out[ch, i] = jnp.dot(lhs[...], w1[i], preferred_element_type=jnp.float32)
            partner[i] = send(part_out.at[ch, i], part_in.at[ch, i], at(dc=1))
        for i in (2, 1, 3, 0):
            if ch == 0:
                w_loads[8 + 2 * i].wait()
                w_loads[8 + 2 * i + 1].wait()
            mine = jnp.dot(lhs[...], w1[4 + i], preferred_element_type=jnp.float32)
            partner[i].wait_recv()
            mine = mine + part_in[ch, i]
            if i == 0:
                own[ch] = mine
            else:
                sum_out[ch, i - 1] = mine.astype(jnp.bfloat16)
                summing[ch].append(send(sum_out.at[ch, i - 1], sum_in.at[ch, i - 1], at(dx=i)))

    def activate(ch):
        for copy in summing[ch]:
            copy.wait_recv()
        total = own[ch]
        for i in range(3):
            total = total + sum_in[ch, i].astype(jnp.float32)
        gate, up = total[:, :128], total[:, 128:]
        hidden = (gate / (1.0 + jnp.exp(-gate)) * up).astype(jnp.bfloat16)
        hid_p[ch, z, y] = hidden[:HALF]
        hid_q[ch, y, z] = hidden[HALF:]
        hp[ch].start()
        hq[ch].start()

    mixing = [None] * CHUNKS
    reducing = [[] for _ in range(CHUNKS)]

    def mix(ch):
        if ch == 0:
            wd_load.wait()
        left = jnp.concatenate([hid_p[ch, a, b] for b in range(NY) for a in range(NZ)], axis=1)
        right = jnp.concatenate([hid_q[ch, b, a] for b in range(NY) for a in range(NZ)], axis=1)
        rows = jnp.concatenate([left, right], axis=0)
        acc[ch] = jnp.dot(rows, wd[...].reshape(NY * NZ * 128, 512), preferred_element_type=jnp.float32)
        theirs = pl.ds(pl.multiple_of((1 - core) * HALF, HALF), HALF)
        mixing[ch] = send(acc.at[ch, theirs], acc_in.at[ch], at(dc=1))

    def scatter(ch):
        mixing[ch].wait_recv()
        for i in (2, 1, 3, 0):
            place = (x + i) % NX * 16
            rows = pl.ds(pl.multiple_of(core * HALF + place, 16), 16)
            total = acc[ch, rows, :] + acc_in[ch, pl.ds(pl.multiple_of(place, 16), 16), :]
            if i == 0:
                acc[ch, rows, :] = total
            else:
                red_out[ch, i - 1] = total.astype(jnp.bfloat16)
                reducing[ch].append(send(red_out.at[ch, i - 1], red_in.at[ch, i - 1], at(dx=i)))

    def finish(ch):
        for copy in reducing[ch]:
            copy.wait_recv()
        rows = pl.ds(pl.multiple_of(core * HALF + x * 16, 16), 16)
        total = acc[ch, rows, :]
        for i in range(3):
            total = total + red_in[ch, i].astype(jnp.float32)
        out_ref[ch * 16:(ch + 1) * 16, :] = total.astype(jnp.bfloat16)

    for ch in range(CHUNKS):
        gp[ch].start()
        gq[ch].start()
    for step in range(1, max(len(gp[0].steps), len(gq[0].steps))):
        for ch in range(CHUNKS):
            gp[ch].advance()
            gq[ch].advance()
    for ch in range(CHUNKS):
        project(ch)
    for t in range(2 * CHUNKS + 7):
        for ch in range(CHUNKS):
            k = t - 2 * ch
            if k == 0:
                activate(ch)
            elif 1 <= k <= 6:
                hp[ch].advance()
                hq[ch].advance()
                if k == 6:
                    mix(ch)
            if k == 7:
                scatter(ch)
                if ch > 0:
                    finish(ch - 1)
    finish(CHUNKS - 1)

    for copy in started:
        copy.wait_send()


def body(tokens, gate_weight, up_weight, down_weight):
    bf16, f32 = jnp.bfloat16, jnp.float32
    return pl.pallas_call(
        kernel,
        out_shape=jax.ShapeDtypeStruct((64, 512), bf16),
        in_specs=[pl.BlockSpec(memory_space=pl.ANY)] * 4,
        out_specs=pl.BlockSpec(memory_space=pltpu.VMEM),
        scratch_shapes=[
            pltpu.VMEM((512, 64), bf16),
            pltpu.VMEM((8, 2048, 256), bf16),
            pltpu.VMEM((32, 128, 512), bf16),
            pltpu.VMEM((CHUNKS, NZ, NY, PK, 128), bf16),
            pltpu.VMEM((CHUNKS, NY, NZ, PK, 128), bf16),
            pltpu.VMEM((ROWS, 2048), bf16),
            pltpu.VMEM((CHUNKS, ROWS, 256), f32),
            pltpu.VMEM((CHUNKS, 4, ROWS, 256), f32),
            pltpu.VMEM((CHUNKS, 4, ROWS, 256), f32),
            pltpu.VMEM((CHUNKS, 3, ROWS, 256), bf16),
            pltpu.VMEM((CHUNKS, 3, ROWS, 256), bf16),
            pltpu.VMEM((CHUNKS, NZ, NY, HALF, 128), bf16),
            pltpu.VMEM((CHUNKS, NY, NZ, HALF, 128), bf16),
            pltpu.VMEM((CHUNKS, ROWS, 512), f32),
            pltpu.VMEM((CHUNKS, HALF, 512), f32),
            pltpu.VMEM((CHUNKS, 3, 16, 512), bf16),
            pltpu.VMEM((CHUNKS, 3, 16, 512), bf16),
            pltpu.SemaphoreType.DMA((18,)),
            pltpu.SemaphoreType.DMA((SEMS,)),
            pltpu.SemaphoreType.DMA((SEMS,)),
        ],
        compiler_params=pltpu.CompilerParams(
            collective_id=0, has_side_effects=True, vmem_limit_bytes=56 * 1024 * 1024
        ),
        cost_estimate=pl.CostEstimate(flops=6442450944, bytes_accessed=12 << 20, transcendentals=0),
    )(tokens, gate_weight, up_weight, down_weight)


def solution(mesh):
    in_specs = (P(None, ("gx", "gy")), P("gx", "gy"), P("gx", "gy"), P(None, "gx", "gy"))
    return jax.shard_map(body, mesh=mesh, in_specs=in_specs, out_specs=P("gx", "gy"), check_vma=False)
```

time: 312 us -> 113 us (0.36)
  waiting for transfers between devices: 277 us -> 0 us
  Pallas kernels: 0 us -> 110 us
  matrix products: 17.1 us -> 0 us
  between operations: 13.1 us -> 0.01 us
  other arithmetic: 3.29 us -> 0 us
    all_gather x2 -> x0, waiting for transfers between devices: 163 us -> none  [the longest x1 82.5 us: body(): lax.all_gather(hidden, 'gy', axis=1, tiled=True)]
    pallas_call x0 -> x1, Pallas kernels: none -> 110 us  [body(): pl.pallas_call(kernel, out_shape=jax.ShapeDtypeStruct((64, 512), bf16), i...]
    psum x1 -> x0, waiting for transfers between devices: 77.3 us -> none  [body(): gate_full, up_full = lax.psum((gate, up), 'gx')]
    reduce_scatter x1 -> x0, waiting for transfers between devices: 35.5 us -> none  [body(): mixed = lax.psum_scatter(partial_out, 'gx', scatter_dimension=0, tiled=True)]
    dot_general x3 -> x0, matrix products: 17.1 us -> none  [the longest x1 6.75 us: body(): jnp.dot(lax.all_gather(hidden, 'gy', axis=1, tiled=True), down_flat, pref...]
    convert_element_type x2 -> x0, other arithmetic: 3.29 us -> none  [the longest x1 1.75 us: body(): hidden = (jax.nn.silu(gate_share) * up_share).astype(jnp.bfloat16)]
  transfers between devices with their start and end apart: 4 -> 0, of which waited for: 4 -> 0; matrix products, arithmetic and copies ran while one was open for 0% -> 0% of each run, Pallas kernels for 0% -> 0%
where the time goes in v1:
time: 113 us
  Pallas kernels  110 us (97%)
  local copies, waits for them, and re-layouts  3.05 us (3%)
    pallas_call x1, Pallas kernels, body(): pl.pallas_call(kernel, out_shape=jax.ShapeDtypeStruct((64, 512), bf16), i...  110 us
    unnamed x2, local copies, waits for them, and re-layouts  3.05 us

profile of v1, /device:TPU:1, one launch (start us, length us, event | category | flops | bytes accessed | tf_op | source)
XLA Modules:
  0.0 112.8 jit_solution(7774932360742239334)
XLA Ops:
  0.0 1.6 %copy.5.tok_hbm = bf16[512,64]{1,0:T(8,128)(2,1)} copy(bf16[512,64]{0,1:T(8,128)(2,1)} %param.4) | data formatting | bytes 131072 | tf_op args[0]
  1.6 109.7 %shard_map.46 = bf16[64,512]{1,0:T(8,128)(2,1)} custom-call(bf16[512,64]{1,0:T(8,128)(2,1)} %copy.5.tok_hbm, bf16[2048,1024]{1,0:T(8,128)(2,1)} %gate_hbm.1, bf16[2048,1024]{1,0:T(8,128)(2,1)} %up_hbm.1, bf16[32,128,512]{2,1,0:T(8,128)(2,1)} %down_hbm.1), custom_call_target="tpu_custom_call" | custom-call | flops 6442450944 | bytes 12582912 | tf_op jit(solution)/shard_map/pallas_call | solution.py:247
  111.3 1.5 %copy.7 = bf16[64,512]{1,0:T(8,128)(2,1)} copy(bf16[64,512]{1,0:T(8,128)(2,1)} %shard_map.46) | data formatting | bytes 131072

commit v2 on v0

v2 whole, which is shorter than its diff:
```python
import jax
import jax.numpy as jnp
from jax import lax
from jax.experimental import pallas as pl
from jax.experimental.pallas import tpu as pltpu
from jax.sharding import PartitionSpec as P

MESH = pl.DeviceIdType.MESH
NX, NC, NY, NZ = 4, 2, 4, 8
CHUNKS = 4
ROWS = 128
HALF = ROWS // 2
TOK_CUTS = (32, 32, 32, 32)
HID_CUTS = (48, 48, 48, 48)


def wrap(d, n):
    d %= n
    return d - n if d > n // 2 else d


def toward(d, n, jump, flip):
    if flip and d == n // 2:
        d = -d
    sign = 1 if d > 0 else -1
    size = abs(d)
    if jump == "all":
        return 0
    if jump == "two":
        return 0 if size <= 2 else sign * 2
    return sign * (size - 1)


def tree(first, jump_y, jump_z):
    parent, stage = {}, {(0, 0): 0}

    def visit(dy, dz):
        if (dy, dz) in stage:
            return stage[dy, dz]
        along_y = (dy != 0) if first == "z" else (dz == 0)
        if along_y:
            up = (wrap(toward(dy, NY, jump_y, dz % 2 == 1), NY), dz)
        else:
            up = (dy, wrap(toward(dz, NZ, jump_z, dy % 2 == 1), NZ))
        parent[dy, dz] = up
        stage[dy, dz] = visit(*up) + 1
        return stage[dy, dz]

    for dy in range(NY):
        for dz in range(NZ):
            visit(wrap(dy, NY), wrap(dz, NZ))
    count = max(stage.values())
    return parent, [sorted((b for b in stage if stage[b] == s), key=lambda b: (-abs(b[0]) - abs(b[1]), b)) for s in range(count + 1)]


def ways(trees):
    groups = {(0, ""): []}
    for part, (parent, stages) in enumerate(trees):
        below = {}
        for block, up in parent.items():
            below.setdefault(up, []).append(block)

        def depth(block):
            return 1 + max([depth(b) for b in below.get(block, [])], default=0)

        for s, blocks in enumerate(stages):
            for block in blocks:
                came = ""
                if s:
                    dy, dz = wrap(parent[block][0] - block[0], NY), wrap(parent[block][1] - block[1], NZ)
                    came = ("y+" if dy > 0 else "y-") if dy else ("z+" if dz > 0 else "z-")
                    if dy == NY // 2:
                        came = "y2"
                nexts = sorted(below.get(block, []), key=lambda b: (-depth(b), b))
                groups.setdefault((s, came), []).append((part, block, nexts))
    keys = sorted(groups)
    return [groups[k] for k in keys], keys


TOK_WAYS = [ways(t) for t in ((tree("y", "all", "two"), tree("z", "all", "two")), (tree("y", "all", "two"), tree("z", "all", "two")), (tree("y", "all", "two"), tree("z", "all", "two")), (tree("y", "all", "two"), tree("z", "all", "two")))]
HID_WAYS = [ways(t) for t in ((tree("y", None, None), tree("z", None, None)), (tree("y", None, None), tree("z", None, None)), (tree("y", None, None), tree("z", None, None)), (tree("y", "all", None), tree("z", "all", None)))]

SHIFTS = {
    (sign * (block[0] - after[0]) % NY, sign * (block[1] - after[1]) % NZ)
    for groups, _ in TOK_WAYS + HID_WAYS for group in groups for _, block, nexts in group for after in nexts for sign in (1, -1)
}
SHIFTS = sorted(SHIFTS)

ORDER = [
    ("tok", 0, 0), ("tok", 1, 0), ("tok", 0, 1), ("tok", 0, 2), ("tok", 0, 4), ("tok", 0, 5),
    ("tok", 0, 3), ("tok", 2, 0), ("tok", 1, 1), ("tok", 1, 2), ("tok", 1, 4), ("tok", 1, 5),
    ("tok", 1, 3), ("tok", 3, 0), ("tok", 0, 6), ("tok", 0, 7), ("tok", 0, 9), ("tok", 2, 1),
    ("tok", 0, 8), ("tok", 0, 10), ("tok", 2, 2), ("tok", 2, 4), ("tok", 2, 3), ("tok", 2, 5),
    ("tok", 1, 6), ("tok", 1, 7), ("tok", 3, 1), ("tok", 1, 8), ("tok", 1, 9), ("tok", 3, 2),
    ("tok", 3, 3), ("tok", 3, 4), ("tok", 1, 10), ("tok", 0, 11), ("tok", 0, 12), ("tok", 0, 14),
    ("tok", 3, 5), ("tok", 0, 13), ("tok", 2, 6), ("tok", 2, 7), ("tok", 0, 15), ("pack", 0, 0),
    ("tok", 2, 8), ("theirs", 0, 2), ("tok", 2, 9), ("theirs", 0, 1), ("theirs", 0, 3), ("theirs", 0, 0),
    ("tok", 1, 11), ("tok", 1, 12), ("tok", 1, 14), ("tok", 2, 10), ("tok", 1, 13), ("tok", 3, 6),
    ("tok", 3, 7), ("mine", 0, 2), ("mine", 0, 1), ("tok", 3, 8), ("tok", 3, 9), ("mine", 0, 3),
    ("mine", 0, 0), ("tok", 1, 15), ("pack", 1, 0), ("theirs", 1, 2), ("tok", 2, 14), ("theirs", 1, 1),
    ("theirs", 1, 3), ("theirs", 1, 0), ("tok", 3, 10), ("tok", 2, 11), ("tok", 2, 12), ("tok", 2, 15),
    ("mine", 1, 2), ("tok", 2, 13), ("pack", 2, 0), ("mine", 1, 1), ("theirs", 2, 2), ("tok", 3, 14),
    ("mine", 1, 3), ("theirs", 2, 1), ("mine", 1, 0), ("theirs", 2, 3), ("act", 0, 0), ("tok", 3, 11),
    ("tok", 3, 12), ("tok", 3, 15), ("theirs", 2, 0), ("mine", 2, 2), ("tok", 3, 13), ("mine", 2, 1),
    ("pack", 3, 0), ("mine", 2, 3), ("theirs", 3, 2), ("theirs", 3, 1), ("theirs", 3, 3), ("mine", 2, 0),
    ("theirs", 3, 0), ("hid", 0, 4), ("hid", 0, 3), ("act", 1, 0), ("hid", 0, 1), ("hid", 0, 2),
    ("mine", 3, 2), ("mine", 3, 1), ("mine", 3, 3), ("mine", 3, 0), ("act", 2, 0), ("hid", 0, 5),
    ("hid", 1, 3), ("hid", 1, 4), ("hid", 0, 7), ("hid", 0, 8), ("hid", 1, 1), ("hid", 1, 2),
    ("hid", 0, 6), ("hid", 2, 4), ("hid", 2, 3), ("act", 3, 0), ("hid", 2, 1), ("hid", 2, 2),
    ("hid", 0, 10), ("hid", 1, 5), ("hid", 1, 7), ("hid", 0, 11), ("hid", 0, 12), ("hid", 0, 9),
    ("hid", 1, 6), ("hid", 1, 8), ("hid", 2, 5), ("hid", 3, 4), ("hid", 3, 5), ("hid", 2, 8),
    ("hid", 2, 7), ("hid", 3, 1), ("hid", 3, 2), ("hid", 3, 3), ("hid", 2, 6), ("hid", 0, 16),
    ("hid", 0, 15), ("hid", 1, 11), ("hid", 0, 13), ("hid", 1, 9), ("hid", 0, 14), ("hid", 1, 12),
    ("hid", 1, 10), ("hid", 3, 9), ("hid", 2, 11), ("hid", 3, 6), ("hid", 3, 7), ("hid", 0, 19),
    ("hid", 3, 10), ("hid", 2, 10), ("hid", 2, 12), ("hid", 0, 20), ("hid", 0, 18), ("hid", 1, 15),
    ("hid", 2, 9), ("hid", 3, 8), ("hid", 1, 16), ("hid", 0, 17), ("hid", 1, 14), ("hid", 1, 13),
    ("hid", 3, 14), ("hid", 2, 15), ("hid", 3, 15), ("hid", 3, 12), ("hid", 1, 19), ("hid", 3, 11),
    ("hid", 2, 13), ("hid", 2, 16), ("hid", 3, 13), ("hid", 0, 22), ("hid", 2, 14), ("hid", 1, 20),
    ("hid", 3, 19), ("hid", 0, 21), ("mix", 0, 0), ("hid", 1, 17), ("hid", 1, 18), ("hid", 2, 19),
    ("hid", 3, 20), ("hid", 3, 16), ("hid", 3, 17), ("hid", 2, 20), ("hid", 1, 22), ("hid", 2, 18),
    ("hid", 3, 24), ("hid", 3, 18), ("scatter", 0, 0), ("hid", 2, 17), ("hid", 3, 25), ("hid", 1, 21),
    ("hid", 2, 22), ("mix", 1, 0), ("hid", 3, 21), ("hid", 3, 22), ("hid", 2, 21), ("hid", 3, 23),
    ("mix", 2, 0), ("mix", 3, 0), ("scatter", 1, 0), ("finish", 0, 0), ("scatter", 2, 0), ("scatter", 3, 0),
    ("finish", 1, 0), ("finish", 2, 0), ("finish", 3, 0),
]


def kernel(
    tok_hbm, gate_hbm, up_hbm, down_hbm, out_ref,
    tok, w1, wd, tok_all, lhs, own, part_out, part_in, sum_out, sum_in,
    hid_all, acc, acc_in, red_out, red_in,
    load_sem, tok_recv, hid_recv, part_recv, sum_recv, mix_recv, red_recv, send_sem,
):
    gx, gy = lax.axis_index("gx"), lax.axis_index("gy")
    x, core, y, z = gx // NC, gx % NC, gy // NZ, gy % NZ

    def at(dx=0, dc=0, dy=0, dz=0):
        return (
            (x + dx + NX) % NX * NC + (core + dc) % NC,
            (y + dy + NY) % NY * NZ + (z + dz + NZ) % NZ,
        )

    def remote(src, dst, sent, received, device):
        return pltpu.make_async_remote_copy(
            src_ref=src, dst_ref=dst, send_sem=sent, recv_sem=received, device_id=device, device_id_type=MESH
        )

    tok_load = pltpu.make_async_copy(tok_hbm, tok, load_sem.at[0])
    tok_load.start()
    barrier = pltpu.get_barrier_semaphore()
    peers = [at(dy=dy, dz=dz) for dy, dz in SHIFTS] + [at(dx=d) for d in (1, 2, 3)] + [at(dc=1)]
    for peer in peers:
        pl.semaphore_signal(barrier, inc=1, device_id=peer, device_id_type=MESH)

    w_wait = {}
    for i in (2, 1, 3, 0, 6, 5, 7, 4):
        share = (x + i % 4) % NX * NC + (core + 1 - i // 4) % NC
        columns = pl.ds(pl.multiple_of(share * 128, 128), 128)
        for h, src in enumerate((gate_hbm, up_hbm)):
            pltpu.make_async_copy(src.at[:, columns], w1.at[i, :, pl.ds(h * 128, 128)], load_sem.at[2 + i]).start()
        w_wait[i] = pltpu.make_async_copy(w1.at[i], w1.at[i], load_sem.at[2 + i])
    wd_load = pltpu.make_async_copy(down_hbm, wd, load_sem.at[1])
    wd_load.start()

    tok_load.wait()
    turned = jnp.swapaxes(tok[...], 0, 1)
    for ch in range(CHUNKS):
        side = []
        for c in range(NC):
            side.append(jnp.concatenate(
                [turned[(i * NC + c) * 64 + ch * 16:(i * NC + c) * 64 + ch * 16 + 16, :] for i in range(NX)], axis=0
            ))
        tok_all[ch, pl.ds(pl.multiple_of(gy * HALF, HALF), HALF)] = jnp.concatenate(side, axis=1)
    pl.semaphore_wait(barrier, len(peers))

    unsent = {}

    def flush(k):
        for copy in unsent.pop(k, ()):
            copy.wait_send()

    class Gather:
        def __init__(self, ref, ch, ways, cut, size, received, k):
            self.ref, self.ch, self.size, self.received, self.k = ref, ch, size, received, k
            self.groups, self.keys = ways
            self.parts = ((0, cut), (cut, size - cut))
            unsent[k] = [self.rows_of((NY * NZ - 1) * size, 0)]

        def rows_of(self, count, g):
            rows = self.ref.at[self.ch, pl.ds(0, count)]
            return remote(rows, rows, send_sem.at[self.k], self.received.at[self.ch, g], at(dy=1))

        def step(self, g):
            group = self.groups[g]
            if g > 0:
                self.rows_of(sum(self.parts[part][1] for part, _, _ in group), g - 1).wait_recv()
            moves = []
            for part, block, nexts in group:
                slot = (y + block[0] + NY) % NY * NZ + (z + block[1] + NZ) % NZ
                first, count = self.parts[part]
                rows = self.ref.at[self.ch, pl.ds(pl.multiple_of(slot * self.size + first, 16), count)]
                for after in nexts:
                    dy, dz = wrap(block[0] - after[0], NY), wrap(block[1] - after[1], NZ)
                    moves.append((rows, at(dy=dy, dz=dz), self.arrives(part, after)))
            for rows, device, there in moves:
                remote(rows, rows, send_sem.at[self.k], self.received.at[self.ch, there - 1], device).start()

        def arrives(self, part, block):
            for g, group in enumerate(self.groups):
                if any(p == part and b == block for p, b, _ in group):
                    return g

    tok_gather = [Gather(tok_all, ch, TOK_WAYS[ch], TOK_CUTS[ch], HALF, tok_recv, ch) for ch in range(CHUNKS)]
    hid_gather = [Gather(hid_all, ch, HID_WAYS[ch], HID_CUTS[ch], ROWS, hid_recv, CHUNKS + ch) for ch in range(CHUNKS)]

    def send_parts(ch, i):
        return remote(part_out.at[ch, i], part_in.at[ch, i], send_sem.at[2 * CHUNKS + ch], part_recv.at[ch, i], at(dc=1))

    def send_sum(ch, i):
        k = 3 * CHUNKS + ch
        return remote(sum_out.at[ch, i - 1], sum_in.at[ch, i - 1], send_sem.at[k], sum_recv.at[ch], at(dx=i))

    def tok_step(ch, s):
        tok_gather[ch].step(s)

    def pack(ch, _):
        for a in range(0, NY * NZ, 2):
            lo, hi = tok_all[ch, a * HALF:(a + 1) * HALF], tok_all[ch, (a + 1) * HALF:(a + 2) * HALF]
            columns = slice(a * 64, a * 64 + 128)
            lhs[ch % 2, :HALF, columns] = jnp.concatenate([lo[:, :64], hi[:, :64]], axis=1)
            lhs[ch % 2, HALF:, columns] = jnp.concatenate([lo[:, 64:], hi[:, 64:]], axis=1)

    def theirs(ch, i):
        if ch == 0:
            w_wait[i].wait()
        part_out[ch, i] = jnp.dot(lhs[ch % 2], w1[i], preferred_element_type=jnp.float32)
        send_parts(ch, i).start()
        if i == 0:
            unsent[2 * CHUNKS + ch] = [remote(part_out.at[ch], part_in.at[ch], send_sem.at[2 * CHUNKS + ch], part_recv.at[ch, i], at(dc=1))]

    def mine(ch, i):
        if ch == 0:
            w_wait[4 + i].wait()
        total = jnp.dot(lhs[ch % 2], w1[4 + i], preferred_element_type=jnp.float32)
        send_parts(ch, i).wait_recv()
        total = total + part_in[ch, i]
        if i == 0:
            own[ch] = total
        else:
            sum_out[ch, i - 1] = total.astype(jnp.bfloat16)
            send_sum(ch, i).start()

    def activate(ch, _):
        k = 3 * CHUNKS + ch
        sums = remote(sum_out.at[ch], sum_in.at[ch], send_sem.at[k], sum_recv.at[ch], at(dx=1))
        unsent[k] = [sums]
        sums.wait_recv()
        total = own[ch]
        for i in range(3):
            total = total + sum_in[ch, i].astype(jnp.float32)
        gate, up = total[:, :128], total[:, 128:]
        hid_all[ch, pl.ds(pl.multiple_of(gy * ROWS, ROWS), ROWS)] = (gate / (1.0 + jnp.exp(-gate)) * up).astype(jnp.bfloat16)
        hid_gather[ch].step(0)

    def hid_step(ch, s):
        hid_gather[ch].step(s)

    def mix(ch, _):
        if ch == 0:
            wd_load.wait()
        rows = jnp.concatenate([hid_all[ch, a * ROWS:(a + 1) * ROWS] for a in range(NY * NZ)], axis=1)
        acc[ch] = jnp.dot(rows, wd[...].reshape(NY * NZ * 128, 512), preferred_element_type=jnp.float32)
        mixed_parts(ch).start()
        unsent[4 * CHUNKS + ch] = [mixed_parts(ch)]

    def mixed_parts(ch):
        part = pl.ds(pl.multiple_of((1 - core) * HALF, HALF), HALF)
        return remote(acc.at[ch, part], acc_in.at[ch], send_sem.at[4 * CHUNKS + ch], mix_recv.at[ch], at(dc=1))

    def scatter(ch, _):
        mixed_parts(ch).wait_recv()
        for i in (2, 1, 3, 0):
            place = (x + i) % NX * 16
            rows = pl.ds(pl.multiple_of(core * HALF + place, 16), 16)
            total = acc[ch, rows, :] + acc_in[ch, pl.ds(pl.multiple_of(place, 16), 16), :]
            if i == 0:
                red_own[ch] = total
            else:
                red_out[ch, i - 1] = total.astype(jnp.bfloat16)
                remote(red_out.at[ch, i - 1], red_in.at[ch, i - 1], send_sem.at[5 * CHUNKS + ch], red_recv.at[ch], at(dx=i)).start()

    red_own = {}

    def finish(ch, _):
        k = 5 * CHUNKS + ch
        parts = remote(red_out.at[ch], red_in.at[ch], send_sem.at[k], red_recv.at[ch], at(dx=1))
        unsent[k] = [parts]
        parts.wait_recv()
        total = red_own[ch]
        for i in range(3):
            total = total + red_in[ch, i].astype(jnp.float32)
        out_ref[ch * 16:(ch + 1) * 16, :] = total.astype(jnp.bfloat16)

    actions = {
        "tok": tok_step, "pack": pack, "theirs": theirs, "mine": mine, "act": activate, "hid": hid_step,
        "mix": mix, "scatter": scatter, "finish": finish,
    }
    for name, ch, step in ORDER:
        actions[name](ch, step)

    for k in list(unsent):
        flush(k)


def body(tokens, gate_weight, up_weight, down_weight):
    bf16, f32 = jnp.bfloat16, jnp.float32
    return pl.pallas_call(
        kernel,
        out_shape=jax.ShapeDtypeStruct((64, 512), bf16),
        in_specs=[pl.BlockSpec(memory_space=pl.ANY)] * 4,
        out_specs=pl.BlockSpec(memory_space=pltpu.VMEM),
        scratch_shapes=[
            pltpu.VMEM((64, 512), bf16),
            pltpu.VMEM((8, 2048, 256), bf16),
            pltpu.VMEM((32, 128, 512), bf16),
            pltpu.VMEM((CHUNKS, NY * NZ * HALF, 128), bf16),
            pltpu.VMEM((2, ROWS, 2048), bf16),
            pltpu.VMEM((CHUNKS, ROWS, 256), f32),
            pltpu.VMEM((CHUNKS, 4, ROWS, 256), f32),
            pltpu.VMEM((CHUNKS, 4, ROWS, 256), f32),
            pltpu.VMEM((CHUNKS, 3, ROWS, 256), bf16),
            pltpu.VMEM((CHUNKS, 3, ROWS, 256), bf16),
            pltpu.VMEM((CHUNKS, NY * NZ * ROWS, 128), bf16),
            pltpu.VMEM((CHUNKS, ROWS, 512), f32),
            pltpu.VMEM((CHUNKS, HALF, 512), f32),
            pltpu.VMEM((CHUNKS, 3, 16, 512), bf16),
            pltpu.VMEM((CHUNKS, 3, 16, 512), bf16),
            pltpu.SemaphoreType.DMA((10,)),
            pltpu.SemaphoreType.DMA((CHUNKS, max(len(w[0]) for w in TOK_WAYS) - 1)),
            pltpu.SemaphoreType.DMA((CHUNKS, max(len(w[0]) for w in HID_WAYS) - 1)),
            pltpu.SemaphoreType.DMA((CHUNKS, 4)),
            pltpu.SemaphoreType.DMA((CHUNKS,)),
            pltpu.SemaphoreType.DMA((CHUNKS,)),
            pltpu.SemaphoreType.DMA((CHUNKS,)),
            pltpu.SemaphoreType.DMA((6 * CHUNKS,)),
        ],
        compiler_params=pltpu.CompilerParams(
            collective_id=0, has_side_effects=True, vmem_limit_bytes=56 * 1024 * 1024
        ),
        cost_estimate=pl.CostEstimate(flops=6442450944, bytes_accessed=12 << 20, transcendentals=0),
    )(tokens.T, gate_weight, up_weight, down_weight)


def solution(mesh):
    in_specs = (P(None, ("gx", "gy")), P("gx", "gy"), P("gx", "gy"), P(None, "gx", "gy"))
    return jax.shard_map(body, mesh=mesh, in_specs=in_specs, out_specs=P("gx", "gy"), check_vma=False)
```

time: 312 us -> 78.4 us (0.25)
  waiting for transfers between devices: 277 us -> 0 us
  Pallas kernels: 0 us -> 76.8 us
  matrix products: 17.1 us -> 0 us
  between operations: 13.1 us -> 0.01 us
  other arithmetic: 3.29 us -> 0 us
    all_gather x2 -> x0, waiting for transfers between devices: 163 us -> none  [the longest x1 82.5 us: body(): lax.all_gather(hidden, 'gy', axis=1, tiled=True)]
    psum x1 -> x0, waiting for transfers between devices: 77.3 us -> none  [body(): gate_full, up_full = lax.psum((gate, up), 'gx')]
    pallas_call x0 -> x1, Pallas kernels: none -> 76.8 us  [body(): pl.pallas_call(kernel, out_shape=jax.ShapeDtypeStruct((64, 512), bf16), i...]
    reduce_scatter x1 -> x0, waiting for transfers between devices: 35.5 us -> none  [body(): mixed = lax.psum_scatter(partial_out, 'gx', scatter_dimension=0, tiled=True)]
    dot_general x3 -> x0, matrix products: 17.1 us -> none  [the longest x1 6.75 us: body(): jnp.dot(lax.all_gather(hidden, 'gy', axis=1, tiled=True), down_flat, pref...]
    convert_element_type x2 -> x0, other arithmetic: 3.29 us -> none  [the longest x1 1.75 us: body(): hidden = (jax.nn.silu(gate_share) * up_share).astype(jnp.bfloat16)]
  transfers between devices with their start and end apart: 4 -> 0, of which waited for: 4 -> 0; matrix products, arithmetic and copies ran while one was open for 0% -> 0% of each run, Pallas kernels for 0% -> 0%
where the time goes in v2:
time: 78.4 us; the launch traced here: 78.3 us
  Pallas kernels  76.8 us (98%)
  local copies, waits for them, and re-layouts  1.47 us (2%)
    pallas_call x1, Pallas kernels, body(): pl.pallas_call(kernel, out_shape=jax.ShapeDtypeStruct((64, 512), bf16), i...  76.8 us

profile of v2, /device:TPU:1, one launch (start us, length us, event | category | flops | bytes accessed | tf_op | source)
XLA Modules:
  0.0 78.3 jit_solution(11044575989591035245)
XLA Ops:
  0.0 76.8 %shard_map.46 = bf16[64,512]{1,0:T(8,128)(2,1)} custom-call(bf16[64,512]{1,0:T(8,128)(2,1)} %bitcast.1, bf16[2048,1024]{1,0:T(8,128)(2,1)} %gate_hbm.1, bf16[2048,1024]{1,0:T(8,128)(2,1)} %up_hbm.1, bf16[32,128,512]{2,1,0:T(8,128)(2,1)} %down_hbm.1), custom_call_target="tpu_custom_call" | custom-call | flops 6442450944 | bytes 12582912 | tf_op jit(solution)/shard_map/pallas_call | solution.py:317
  76.8 1.5 %copy.6 = bf16[64,512]{1,0:T(8,128)(2,1)} copy(bf16[64,512]{1,0:T(8,128)(2,1)} %shard_map.46) | data formatting | bytes 131072

commit v3 on v2

v3 whole, which is shorter than its diff:
```python
import jax
import jax.numpy as jnp
from jax import lax
from jax.experimental import pallas as pl
from jax.experimental.pallas import tpu as pltpu
from jax.sharding import PartitionSpec as P

MESH = pl.DeviceIdType.MESH
NX, NC, NY, NZ = 4, 2, 4, 8
CHUNKS = 4
ROWS = 128
HALF = ROWS // 2
TOK_CUTS = (16, 16, 32, 16)
HID_CUTS = (32, 48, 32, 64)


def wrap(d, n):
    d %= n
    return d - n if d > n // 2 else d


def place(i):
    return wrap(i // NZ, NY), wrap(i % NZ, NZ)


def tree(parents):
    parent = {place(i): place(up) for i, up in enumerate(parents) if i}
    stage = {(0, 0): 0}

    def visit(block):
        if block not in stage:
            stage[block] = visit(parent[block]) + 1
        return stage[block]

    for block in parent:
        visit(block)
    return parent, [[block for block in stage if stage[block] == s] for s in range(max(stage.values()) + 1)]


def depth_of(parent, block):
    return 1 + max([depth_of(parent, b) for b, up in parent.items() if up == block], default=0)


def ways(trees):
    groups = {(0, ""): []}
    for part, (parent, stages) in enumerate(trees):
        below = {}
        for block, up in parent.items():
            below.setdefault(up, []).append(block)

        for s, blocks in enumerate(stages):
            for block in blocks:
                came = ""
                if s:
                    dy, dz = wrap(parent[block][0] - block[0], NY), wrap(parent[block][1] - block[1], NZ)
                    came = ("y+" if dy > 0 else "y-") if dy else ("z+" if dz > 0 else "z-")
                    if dy == NY // 2:
                        came = "y2"
                nexts = sorted(below.get(block, []), key=lambda b: (-depth_of(parent, b), b))
                groups.setdefault((s, came), []).append((part, block, nexts))
    keys = sorted(groups)
    return [groups[k] for k in keys], [parent for parent, _ in trees]


PARENTS = (
    (0, 0, 0, 2, 2, 6, 0, 0, 0, 1, 8, 9, 15, 5, 6, 8, 0, 25, 10, 27, 21, 16, 30, 15, 0, 24, 24, 24, 27, 5, 24, 24),
    (0, 0, 0, 1, 6, 6, 0, 0, 0, 1, 2, 3, 4, 15, 6, 7, 24, 9, 2, 18, 4, 5, 16, 16, 0, 24, 2, 26, 4, 5, 31, 24),
    (0, 0, 0, 2, 1, 6, 0, 0, 0, 1, 8, 9, 4, 5, 15, 7, 24, 25, 10, 3, 16, 5, 30, 31, 0, 1, 2, 24, 4, 31, 6, 7),
    (0, 0, 0, 1, 2, 6, 0, 0, 0, 1, 2, 9, 14, 14, 6, 7, 0, 25, 2, 3, 4, 5, 30, 16, 0, 1, 2, 26, 4, 31, 6, 7),
    (0, 0, 0, 0, 2, 6, 7, 0, 0, 1, 9, 3, 10, 15, 6, 7, 8, 16, 16, 11, 4, 23, 6, 15, 0, 1, 25, 3, 27, 24, 31, 7),
    (0, 0, 0, 2, 1, 6, 0, 0, 0, 8, 8, 3, 4, 15, 6, 8, 8, 9, 16, 17, 4, 5, 14, 15, 0, 1, 2, 26, 30, 30, 24, 24),
    (0, 0, 0, 0, 1, 0, 0, 0, 0, 1, 8, 10, 4, 15, 15, 7, 24, 25, 2, 3, 19, 16, 16, 31, 0, 24, 24, 25, 24, 24, 31, 24),
    (0, 0, 0, 1, 2, 7, 0, 0, 0, 8, 2, 9, 4, 5, 6, 8, 8, 16, 2, 3, 4, 23, 14, 7, 0, 1, 2, 26, 4, 24, 31, 24),
    (0, 0, 0, 2, 2, 6, 0, 0, 0, 1, 2, 3, 4, 14, 8, 8, 0, 25, 10, 18, 4, 29, 14, 16, 0, 1, 2, 3, 26, 30, 6, 7),
    (0, 0, 0, 2, 2, 6, 0, 0, 0, 1, 2, 10, 4, 5, 6, 8, 0, 16, 10, 11, 12, 29, 6, 31, 0, 24, 2, 3, 4, 5, 6, 7),
    (0, 0, 0, 0, 3, 6, 0, 0, 0, 8, 2, 3, 11, 14, 15, 8, 0, 25, 10, 27, 12, 29, 14, 31, 0, 24, 2, 3, 4, 30, 31, 7),
    (0, 0, 1, 2, 5, 0, 7, 0, 0, 1, 9, 10, 11, 5, 8, 8, 0, 25, 26, 18, 28, 22, 14, 15, 0, 1, 25, 3, 4, 5, 31, 24),
    (0, 0, 1, 2, 5, 7, 7, 0, 0, 8, 9, 3, 4, 14, 15, 8, 8, 25, 17, 27, 28, 23, 23, 16, 0, 1, 24, 26, 26, 5, 6, 7),
    (0, 0, 0, 2, 2, 6, 7, 0, 0, 1, 2, 3, 4, 5, 6, 8, 8, 16, 10, 11, 28, 5, 14, 15, 0, 1, 25, 26, 4, 30, 31, 24),
    (0, 0, 1, 2, 5, 7, 7, 0, 0, 1, 2, 10, 13, 5, 15, 8, 8, 16, 26, 3, 17, 13, 23, 16, 0, 24, 2, 26, 29, 5, 31, 24),
    (0, 0, 0, 2, 2, 6, 0, 0, 0, 1, 2, 3, 4, 15, 15, 8, 24, 25, 10, 27, 12, 29, 30, 16, 0, 1, 2, 26, 27, 5, 6, 7),
)
TOK_WAYS = [ways([tree(PARENTS[i]) for i in pair]) for pair in ((0, 1), (2, 3), (4, 5), (6, 7))]
HID_WAYS = [ways([tree(PARENTS[i]) for i in pair]) for pair in ((8, 9), (10, 11), (12, 13), (14, 15))]

SHIFTS = {
    (sign * (block[0] - after[0]) % NY, sign * (block[1] - after[1]) % NZ)
    for groups, _ in TOK_WAYS + HID_WAYS for group in groups for _, block, nexts in group for after in nexts for sign in (1, -1)
}
SHIFTS = sorted(SHIFTS)

LHS = (0, 1, 0, 1)

ORDER = [
    ("tok", 0, 0), ("tok", 1, 0), ("tok", 2, 0), ("tok", 0, 1), ("tok", 0, 2), ("tok", 0, 3),
    ("tok", 0, 4), ("tok", 0, 5), ("tok", 1, 1), ("tok", 1, 2), ("tok", 1, 3), ("tok", 1, 4),
    ("tok", 1, 5), ("tok", 2, 1), ("tok", 2, 2), ("tok", 2, 3), ("tok", 2, 4), ("tok", 0, 6),
    ("tok", 0, 9), ("tok", 0, 7), ("tok", 0, 10), ("tok", 0, 8), ("tok", 1, 9), ("tok", 3, 0),
    ("tok", 1, 6), ("tok", 1, 7), ("tok", 1, 10), ("tok", 1, 8), ("tok", 2, 5), ("tok", 2, 7),
    ("tok", 2, 6), ("tok", 0, 15), ("tok", 2, 8), ("tok", 0, 11), ("tok", 0, 12), ("tok", 0, 13),
    ("tok", 0, 14), ("pack", 0, 0), ("theirs", 0, 2), ("tok", 3, 1), ("tok", 3, 2), ("tok", 1, 12),
    ("theirs", 0, 1), ("tok", 3, 4), ("theirs", 0, 3), ("tok", 3, 3), ("theirs", 0, 0), ("tok", 1, 11),
    ("tok", 1, 15), ("mine", 0, 2), ("tok", 1, 13), ("tok", 1, 14), ("pack", 1, 0), ("theirs", 1, 2),
    ("mine", 0, 1), ("tok", 2, 9), ("mine", 0, 3), ("tok", 2, 12), ("theirs", 1, 1), ("mine", 0, 0),
    ("tok", 2, 10), ("theirs", 1, 3), ("tok", 2, 11), ("theirs", 1, 0), ("tok", 3, 5), ("mine", 1, 2),
    ("tok", 3, 6), ("tok", 3, 9), ("mine", 1, 1), ("mine", 1, 3), ("tok", 3, 7), ("tok", 3, 8),
    ("mine", 1, 0), ("tok", 2, 13), ("tok", 2, 14), ("pack", 2, 0), ("theirs", 2, 2), ("theirs", 2, 1),
    ("theirs", 2, 3), ("theirs", 2, 0), ("act", 0, 0), ("mine", 2, 2), ("tok", 3, 10), ("tok", 3, 14),
    ("tok", 3, 11), ("mine", 2, 1), ("tok", 3, 12), ("tok", 3, 13), ("pack", 3, 0), ("mine", 2, 3),
    ("act", 1, 0), ("mine", 2, 0), ("theirs", 3, 2), ("theirs", 3, 1), ("theirs", 3, 3), ("hid", 0, 2),
    ("theirs", 3, 0), ("hid", 0, 5), ("hid", 0, 1), ("hid", 0, 4), ("hid", 0, 3), ("mine", 3, 2),
    ("mine", 3, 1), ("hid", 1, 2), ("hid", 1, 1), ("mine", 3, 3), ("act", 2, 0), ("mine", 3, 0),
    ("hid", 1, 5), ("hid", 1, 3), ("hid", 1, 4), ("hid", 0, 7), ("hid", 0, 9), ("hid", 0, 10),
    ("hid", 0, 6), ("hid", 0, 8), ("hid", 2, 2), ("hid", 2, 1), ("act", 3, 0), ("hid", 2, 3),
    ("hid", 1, 7), ("hid", 1, 6), ("hid", 2, 4), ("hid", 1, 8), ("hid", 1, 9), ("hid", 0, 14),
    ("hid", 0, 12), ("hid", 0, 15), ("hid", 0, 11), ("hid", 0, 13), ("hid", 3, 1), ("hid", 3, 2),
    ("hid", 3, 4), ("hid", 3, 3), ("hid", 2, 7), ("hid", 2, 6), ("hid", 2, 5), ("hid", 1, 12),
    ("hid", 1, 11), ("hid", 1, 10), ("hid", 1, 13), ("hid", 0, 17), ("hid", 0, 18), ("hid", 0, 16),
    ("hid", 2, 8), ("mix", 0, 0), ("hid", 3, 6), ("hid", 3, 7), ("hid", 3, 5), ("hid", 3, 8),
    ("hid", 2, 11), ("hid", 1, 17), ("hid", 1, 15), ("hid", 1, 14), ("hid", 1, 16), ("hid", 2, 9),
    ("hid", 2, 10), ("hid", 2, 12), ("hid", 3, 12), ("finish", 0, 0), ("hid", 3, 10), ("hid", 3, 9),
    ("hid", 1, 19), ("hid", 3, 11), ("hid", 1, 18), ("mix", 1, 0), ("hid", 2, 13), ("hid", 2, 15),
    ("hid", 2, 16), ("hid", 2, 17), ("hid", 2, 14), ("mix", 2, 0), ("hid", 3, 15), ("hid", 3, 16),
    ("hid", 3, 14), ("hid", 3, 17), ("hid", 3, 13), ("mix", 3, 0), ("finish", 1, 0), ("finish", 2, 0),
    ("finish", 3, 0),
]


def kernel(
    tok_hbm, gate_hbm, up_hbm, down_hbm, out_ref,
    tok, w1, wd, tok_all, lhs, own, part_out, part_in, sum_out, sum_in,
    hid_all, acc, red_out, red_in,
    load_sem, tok_recv, hid_recv, part_recv, sum_recv, red_recv, send_sem,
):
    gx, gy = lax.axis_index("gx"), lax.axis_index("gy")
    x, core, y, z = gx // NC, gx % NC, gy // NZ, gy % NZ

    xs = [(x + d) % NX * NC for d in range(NX)]
    cores = [core, 1 - core]
    ys = [(y + d) % NY * NZ for d in range(NY)]
    zs = [(z + d) % NZ for d in range(NZ)]
    places = {}

    def slot_of(dy, dz):
        key = (dy % NY, dz % NZ)
        if key not in places:
            places[key] = ys[key[0]] + zs[key[1]] if any(key) else gy
        return places[key]

    def at(dx=0, dc=0, dy=0, dz=0):
        return (xs[dx % NX] + cores[dc % NC] if dx % NX or dc % NC else gx, slot_of(dy, dz))

    def remote(src, dst, sent, received, device):
        return pltpu.make_async_remote_copy(
            src_ref=src, dst_ref=dst, send_sem=sent, recv_sem=received, device_id=device, device_id_type=MESH
        )

    tok_load = pltpu.make_async_copy(tok_hbm, tok, load_sem.at[0])
    tok_load.start()
    barrier = pltpu.get_barrier_semaphore()
    peers = [at(dy=dy, dz=dz) for dy, dz in SHIFTS] + [at(dx=dx, dc=dc) for dx in range(NX) for dc in range(NC) if dx + dc]
    for peer in peers:
        pl.semaphore_signal(barrier, inc=1, device_id=peer, device_id_type=MESH)

    w_wait = {}
    for i in (2, 1, 3, 0, 6, 5, 7, 4):
        share = at(dx=i % 4, dc=1 - i // 4)[0]
        columns = pl.ds(pl.multiple_of(share * 128, 128), 128)
        for h, src in enumerate((gate_hbm, up_hbm)):
            pltpu.make_async_copy(src.at[:, columns], w1.at[i, :, pl.ds(h * 128, 128)], load_sem.at[2 + i]).start()
        w_wait[i] = pltpu.make_async_copy(w1.at[i], w1.at[i], load_sem.at[2 + i])
    wd_load = pltpu.make_async_copy(down_hbm, wd, load_sem.at[1])
    wd_load.start()

    tok_load.wait()
    turned = jnp.swapaxes(tok[...], 0, 1)
    for ch in range(CHUNKS):
        side = []
        for c in range(NC):
            side.append(jnp.concatenate(
                [turned[(i * NC + c) * 64 + ch * 16:(i * NC + c) * 64 + ch * 16 + 16, :] for i in range(NX)], axis=0
            ))
        tok_all[ch, pl.ds(pl.multiple_of(gy * HALF, HALF), HALF)] = jnp.concatenate(side, axis=1)
    pl.semaphore_wait(barrier, len(peers))

    unsent = {}

    def flush(k):
        for copy in unsent.pop(k, ()):
            copy.wait_send()

    class Gather:
        def __init__(self, ref, ch, ways, cut, size, received, k):
            self.ref, self.ch, self.size, self.received, self.k = ref, ch, size, received, k
            self.groups, self.trees = ways
            self.parts = ((0, cut), (cut, size - cut))

        def rows_of(self, count, g):
            rows = self.ref.at[self.ch, pl.ds(0, count)]
            return remote(rows, rows, send_sem.at[self.k], self.received.at[self.ch, g], at(dy=1))

        def step(self, g):
            group = self.groups[g]
            if g == 0:
                unsent[self.k] = [self.rows_of((NY * NZ - 1) * self.size, 0)]
            else:
                self.rows_of(sum(self.parts[part][1] for part, _, _ in group), g - 1).wait_recv()
            moves = []
            for part, block, nexts in group:
                slot = slot_of(*block)
                first, count = self.parts[part]
                rows = self.ref.at[self.ch, pl.ds(pl.multiple_of(slot * self.size + first, 16), count)]
                for after in nexts:
                    dy, dz = wrap(block[0] - after[0], NY), wrap(block[1] - after[1], NZ)
                    moves.append((-depth_of(self.trees[part], after), rows, at(dy=dy, dz=dz), self.arrives(part, after)))
            moves.sort(key=lambda move: move[0])
            for _, rows, device, there in moves:
                remote(rows, rows, send_sem.at[self.k], self.received.at[self.ch, there - 1], device).start()

        def arrives(self, part, block):
            for g, group in enumerate(self.groups):
                if any(p == part and b == block for p, b, _ in group):
                    return g

    tok_gather = [Gather(tok_all, ch, TOK_WAYS[ch], TOK_CUTS[ch], HALF, tok_recv, ch) for ch in range(CHUNKS)]
    hid_gather = [Gather(hid_all, ch, HID_WAYS[ch], HID_CUTS[ch], ROWS, hid_recv, CHUNKS + ch) for ch in range(CHUNKS)]

    def send_parts(ch, i):
        return remote(part_out.at[ch, i], part_in.at[ch, i], send_sem.at[2 * CHUNKS + ch], part_recv.at[ch, i], at(dc=1))

    def send_sum(ch, i):
        k = 3 * CHUNKS + ch
        return remote(sum_out.at[ch, i - 1], sum_in.at[ch, i - 1], send_sem.at[k], sum_recv.at[ch], at(dx=i))

    def tok_step(ch, s):
        tok_gather[ch].step(s)

    def pack(ch, _):
        for a in range(0, NY * NZ, 2):
            lo, hi = tok_all[ch, a * HALF:(a + 1) * HALF], tok_all[ch, (a + 1) * HALF:(a + 2) * HALF]
            columns = slice(a * 64, a * 64 + 128)
            lhs[LHS[ch], :HALF, columns] = jnp.concatenate([lo[:, :64], hi[:, :64]], axis=1)
            lhs[LHS[ch], HALF:, columns] = jnp.concatenate([lo[:, 64:], hi[:, 64:]], axis=1)

    def theirs(ch, i):
        if ch == 0:
            w_wait[i].wait()
        part_out[ch, i] = jnp.dot(lhs[LHS[ch]], w1[i], preferred_element_type=jnp.float32)
        send_parts(ch, i).start()
        if i == 0:
            unsent[2 * CHUNKS + ch] = [remote(part_out.at[ch], part_in.at[ch], send_sem.at[2 * CHUNKS + ch], part_recv.at[ch, i], at(dc=1))]

    def mine(ch, i):
        if ch == 0:
            w_wait[4 + i].wait()
        total = jnp.dot(lhs[LHS[ch]], w1[4 + i], preferred_element_type=jnp.float32)
        send_parts(ch, i).wait_recv()
        total = total + part_in[ch, i]
        if i == 0:
            own[ch] = total
        else:
            sum_out[ch, i - 1] = total.astype(jnp.bfloat16)
            send_sum(ch, i).start()

    def activate(ch, _):
        k = 3 * CHUNKS + ch
        sums = remote(sum_out.at[ch], sum_in.at[ch], send_sem.at[k], sum_recv.at[ch], at(dx=1))
        unsent[k] = [sums]
        sums.wait_recv()
        total = own[ch]
        for i in range(3):
            total = total + sum_in[ch, i].astype(jnp.float32)
        gate, up = total[:, :128], total[:, 128:]
        hid_all[ch, pl.ds(pl.multiple_of(gy * ROWS, ROWS), ROWS)] = (gate / (1.0 + jnp.exp(-gate)) * up).astype(jnp.bfloat16)
        hid_gather[ch].step(0)

    def hid_step(ch, s):
        hid_gather[ch].step(s)

    def mix(ch, _):
        if ch == 0:
            wd_load.wait()
        rows = jnp.concatenate([hid_all[ch, a * ROWS:(a + 1) * ROWS] for a in range(NY * NZ)], axis=1)
        total = jnp.dot(rows, wd[...].reshape(NY * NZ * 128, 512), preferred_element_type=jnp.float32)
        acc[ch] = total
        red_out[ch] = total.astype(jnp.bfloat16)
        for k, (dx, dc) in enumerate(((2, 0), (2, 1), (1, 0), (1, 1), (3, 0), (3, 1), (0, 1))):
            place = (core + dc) % NC * HALF + (x + dx) % NX * 16
            part = red_out.at[ch, pl.ds(pl.multiple_of(place, 16), 16)]
            there = red_in.at[ch, pl.ds(k * 16, 16)]
            remote(part, there, send_sem.at[4 * CHUNKS + ch], red_recv.at[ch], at(dx=dx, dc=dc)).start()
        unsent[4 * CHUNKS + ch] = [all_reduced(ch)]

    def all_reduced(ch):
        return remote(red_out.at[ch, pl.ds(0, 7 * 16)], red_in.at[ch], send_sem.at[4 * CHUNKS + ch], red_recv.at[ch], at(dc=1))

    def finish(ch, _):
        all_reduced(ch).wait_recv()
        total = acc[ch, pl.ds(pl.multiple_of(core * HALF + x * 16, 16), 16), :]
        for k in range(7):
            total = total + red_in[ch, k * 16:(k + 1) * 16].astype(jnp.float32)
        out_ref[ch * 16:(ch + 1) * 16, :] = total.astype(jnp.bfloat16)

    actions = {
        "tok": tok_step, "pack": pack, "theirs": theirs, "mine": mine, "act": activate, "hid": hid_step,
        "mix": mix, "finish": finish,
    }
    for name, ch, step in ORDER:
        actions[name](ch, step)

    for k in list(unsent):
        flush(k)


def body(tokens, gate_weight, up_weight, down_weight):
    bf16, f32 = jnp.bfloat16, jnp.float32
    return pl.pallas_call(
        kernel,
        out_shape=pltpu.VMEM((64, 512), bf16),
        in_specs=[pl.BlockSpec(memory_space=pl.ANY)] * 4,
        out_specs=pl.BlockSpec(memory_space=pltpu.VMEM),
        scratch_shapes=[
            pltpu.VMEM((64, 512), bf16),
            pltpu.VMEM((8, 2048, 256), bf16),
            pltpu.VMEM((32, 128, 512), bf16),
            pltpu.VMEM((CHUNKS, NY * NZ * HALF, 128), bf16),
            pltpu.VMEM((2, ROWS, 2048), bf16),
            pltpu.VMEM((CHUNKS, ROWS, 256), f32),
            pltpu.VMEM((CHUNKS, 4, ROWS, 256), f32),
            pltpu.VMEM((CHUNKS, 4, ROWS, 256), f32),
            pltpu.VMEM((CHUNKS, 3, ROWS, 256), bf16),
            pltpu.VMEM((CHUNKS, 3, ROWS, 256), bf16),
            pltpu.VMEM((CHUNKS, NY * NZ * ROWS, 128), bf16),
            pltpu.VMEM((CHUNKS, ROWS, 512), f32),
            pltpu.VMEM((CHUNKS, ROWS, 512), bf16),
            pltpu.VMEM((CHUNKS, 7 * 16, 512), bf16),
            pltpu.SemaphoreType.DMA((10,)),
            pltpu.SemaphoreType.DMA((CHUNKS, max(len(w[0]) for w in TOK_WAYS) - 1)),
            pltpu.SemaphoreType.DMA((CHUNKS, max(len(w[0]) for w in HID_WAYS) - 1)),
            pltpu.SemaphoreType.DMA((CHUNKS, 4)),
            pltpu.SemaphoreType.DMA((CHUNKS,)),
            pltpu.SemaphoreType.DMA((CHUNKS,)),
            pltpu.SemaphoreType.DMA((5 * CHUNKS,)),
        ],
        compiler_params=pltpu.CompilerParams(
            collective_id=0, has_side_effects=True, vmem_limit_bytes=56 * 1024 * 1024
        ),
        cost_estimate=pl.CostEstimate(flops=6442450944, bytes_accessed=12 << 20, transcendentals=0),
    )(tokens.T, gate_weight, up_weight, down_weight)


def solution(mesh):
    in_specs = (P(None, ("gx", "gy")), P("gx", "gy"), P("gx", "gy"), P(None, "gx", "gy"))
    return jax.shard_map(body, mesh=mesh, in_specs=in_specs, out_specs=P("gx", "gy"), check_vma=False)
```

time: 78.4 us -> 70.8 us (0.903)
  Pallas kernels: 76.8 us -> 70 us
  local copies, waits for them, and re-layouts: 1.47 us -> 0.63 us
    pallas_call x1, Pallas kernels: 76.8 us -> 70 us  [body(): pl.pallas_call(kernel, out_shape=pltpu.VMEM((64, 512), bf16), in_specs=[p...]
    unnamed x1, local copies, waits for them, and re-layouts: 1.47 us -> 0.63 us
where the time goes in v3:
time: 70.8 us; the launch traced here: 70.7 us
  Pallas kernels  70 us (99%)
    pallas_call x1, Pallas kernels, body(): pl.pallas_call(kernel, out_shape=pltpu.VMEM((64, 512), bf16), in_specs=[p...  70 us

profile of v3, /device:TPU:1, one launch (start us, length us, event | category | flops | bytes accessed | tf_op | source)
XLA Modules:
  0.0 70.7 jit_solution(18057681417907210160)
XLA Ops:
  0.0 70.0 %shard_map.46 = bf16[64,512]{1,0:T(8,128)(2,1)S(1)} custom-call(bf16[64,512]{1,0:T(8,128)(2,1)} %bitcast.1, bf16[2048,1024]{1,0:T(8,128)(2,1)} %gate_hbm.1, bf16[2048,1024]{1,0:T(8,128)(2,1)} %up_hbm.1, bf16[32,128,512]{2,1,0:T(8,128)(2,1)} %down_hbm.1), custom_call_target="tpu_custom_call" | custom-call | flops 6442450944 | bytes 12582912 | tf_op jit(solution)/shard_map/pallas_call | solution.py:317
  70.1 0.6 copy.6

commit v4 on v3

--- a/solution.py
+++ b/solution.py
@@ -10,8 +10,8 @@
 CHUNKS = 4
 ROWS = 128
 HALF = ROWS // 2
-TOK_CUTS = (16, 16, 32, 16)
-HID_CUTS = (32, 48, 32, 64)
+TOK_CUTS = (16, 16, 48, 48)
+HID_CUTS = (32, 32, 32, 80)
 
 
 def wrap(d, n):
@@ -63,26 +63,28 @@
 
 
 PARENTS = (
-    (0, 0, 0, 2, 2, 6, 0, 0, 0, 1, 8, 9, 15, 5, 6, 8, 0, 25, 10, 27, 21, 16, 30, 15, 0, 24, 24, 24, 27, 5, 24, 24),
-    (0, 0, 0, 1, 6, 6, 0, 0, 0, 1, 2, 3, 4, 15, 6, 7, 24, 9, 2, 18, 4, 5, 16, 16, 0, 24, 2, 26, 4, 5, 31, 24),
-    (0, 0, 0, 2, 1, 6, 0, 0, 0, 1, 8, 9, 4, 5, 15, 7, 24, 25, 10, 3, 16, 5, 30, 31, 0, 1, 2, 24, 4, 31, 6, 7),
-    (0, 0, 0, 1, 2, 6, 0, 0, 0, 1, 2, 9, 14, 14, 6, 7, 0, 25, 2, 3, 4, 5, 30, 16, 0, 1, 2, 26, 4, 31, 6, 7),
-    (0, 0, 0, 0, 2, 6, 7, 0, 0, 1, 9, 3, 10, 15, 6, 7, 8, 16, 16, 11, 4, 23, 6, 15, 0, 1, 25, 3, 27, 24, 31, 7),
-    (0, 0, 0, 2, 1, 6, 0, 0, 0, 8, 8, 3, 4, 15, 6, 8, 8, 9, 16, 17, 4, 5, 14, 15, 0, 1, 2, 26, 30, 30, 24, 24),
-    (0, 0, 0, 0, 1, 0, 0, 0, 0, 1, 8, 10, 4, 15, 15, 7, 24, 25, 2, 3, 19, 16, 16, 31, 0, 24, 24, 25, 24, 24, 31, 24),
-    (0, 0, 0, 1, 2, 7, 0, 0, 0, 8, 2, 9, 4, 5, 6, 8, 8, 16, 2, 3, 4, 23, 14, 7, 0, 1, 2, 26, 4, 24, 31, 24),
-    (0, 0, 0, 2, 2, 6, 0, 0, 0, 1, 2, 3, 4, 14, 8, 8, 0, 25, 10, 18, 4, 29, 14, 16, 0, 1, 2, 3, 26, 30, 6, 7),
-    (0, 0, 0, 2, 2, 6, 0, 0, 0, 1, 2, 10, 4, 5, 6, 8, 0, 16, 10, 11, 12, 29, 6, 31, 0, 24, 2, 3, 4, 5, 6, 7),
-    (0, 0, 0, 0, 3, 6, 0, 0, 0, 8, 2, 3, 11, 14, 15, 8, 0, 25, 10, 27, 12, 29, 14, 31, 0, 24, 2, 3, 4, 30, 31, 7),
-    (0, 0, 1, 2, 5, 0, 7, 0, 0, 1, 9, 10, 11, 5, 8, 8, 0, 25, 26, 18, 28, 22, 14, 15, 0, 1, 25, 3, 4, 5, 31, 24),
-    (0, 0, 1, 2, 5, 7, 7, 0, 0, 8, 9, 3, 4, 14, 15, 8, 8, 25, 17, 27, 28, 23, 23, 16, 0, 1, 24, 26, 26, 5, 6, 7),
-    (0, 0, 0, 2, 2, 6, 7, 0, 0, 1, 2, 3, 4, 5, 6, 8, 8, 16, 10, 11, 28, 5, 14, 15, 0, 1, 25, 26, 4, 30, 31, 24),
-    (0, 0, 1, 2, 5, 7, 7, 0, 0, 1, 2, 10, 13, 5, 15, 8, 8, 16, 26, 3, 17, 13, 23, 16, 0, 24, 2, 26, 29, 5, 31, 24),
-    (0, 0, 0, 2, 2, 6, 0, 0, 0, 1, 2, 3, 4, 15, 15, 8, 24, 25, 10, 27, 12, 29, 30, 16, 0, 1, 2, 26, 27, 5, 6, 7),
+    (0, 0, 0, 2, 6, 6, 0, 0, 0, 8, 2, 8, 10, 8, 6, 8, 8, 1, 2, 18, 4, 29, 30, 15, 0, 1, 2, 26, 4, 24, 6, 7),
+    (0, 0, 0, 2, 2, 6, 0, 0, 0, 1, 2, 10, 4, 14, 8, 7, 8, 16, 26, 3, 4, 22, 6, 15, 0, 24, 2, 26, 26, 30, 6, 7),
+    (0, 0, 0, 0, 6, 6, 0, 0, 0, 1, 8, 10, 4, 14, 6, 8, 0, 25, 16, 18, 18, 5, 30, 16, 0, 1, 2, 3, 25, 31, 6, 7),
+    (0, 0, 0, 1, 2, 6, 0, 0, 0, 1, 9, 3, 4, 5, 8, 7, 0, 9, 26, 3, 4, 22, 6, 15, 0, 1, 2, 3, 30, 5, 6, 7),
+    (0, 0, 0, 2, 5, 7, 0, 0, 0, 1, 9, 3, 4, 14, 6, 8, 8, 25, 2, 11, 12, 13, 23, 15, 0, 1, 25, 25, 26, 30, 6, 7),
+    (0, 0, 1, 1, 1, 0, 0, 0, 0, 1, 2, 10, 14, 5, 15, 7, 24, 9, 10, 11, 17, 23, 16, 16, 0, 1, 2, 26, 26, 30, 24, 24),
+    (0, 0, 0, 2, 6, 6, 0, 0, 0, 8, 2, 3, 9, 15, 15, 7, 8, 9, 26, 3, 22, 22, 6, 15, 0, 1, 2, 3, 4, 24, 31, 7),
+    (0, 0, 0, 2, 1, 7, 0, 0, 0, 1, 8, 10, 15, 5, 6, 8, 0, 16, 10, 17, 22, 22, 16, 15, 0, 24, 2, 3, 25, 30, 6, 7),
+    (0, 0, 1, 2, 2, 6, 0, 0, 0, 8, 8, 10, 14, 15, 6, 8, 24, 9, 2, 11, 18, 22, 16, 15, 0, 1, 2, 3, 4, 30, 24, 24),
+    (0, 0, 0, 0, 6, 6, 0, 0, 0, 8, 2, 9, 11, 5, 15, 7, 0, 16, 2, 3, 19, 22, 6, 15, 0, 24, 2, 3, 4, 30, 6, 7),
+    (0, 0, 1, 1, 3, 6, 7, 0, 0, 1, 9, 10, 4, 5, 8, 8, 24, 9, 26, 18, 18, 13, 23, 15, 0, 24, 25, 26, 27, 30, 31, 24),
+    (0, 0, 1, 2, 3, 6, 7, 0, 0, 1, 2, 10, 4, 5, 15, 7, 8, 25, 10, 18, 4, 22, 30, 31, 0, 1, 2, 3, 29, 30, 6, 7),
+    (0, 0, 1, 2, 5, 6, 0, 0, 0, 8, 2, 9, 14, 5, 6, 8, 0, 25, 17, 11, 21, 5, 30, 31, 0, 24, 2, 26, 4, 30, 31, 24),
+    (0, 0, 1, 2, 5, 6, 0, 0, 0, 8, 2, 3, 13, 14, 6, 7, 8, 16, 26, 17, 22, 13, 14, 31, 0, 1, 2, 26, 4, 30, 6, 7),
+    (0, 0, 1, 0, 5, 6, 7, 0, 0, 1, 2, 3, 10, 14, 6, 7, 8, 25, 10, 11, 28, 5, 23, 16, 0, 1, 25, 3, 27, 5, 6, 7),
+    (0, 0, 1, 2, 5, 6, 0, 0, 0, 8, 2, 3, 4, 5, 6, 7, 24, 16, 10, 3, 17, 29, 30, 16, 0, 1, 2, 26, 4, 5, 31, 24),
 )
 TOK_WAYS = [ways([tree(PARENTS[i]) for i in pair]) for pair in ((0, 1), (2, 3), (4, 5), (6, 7))]
 HID_WAYS = [ways([tree(PARENTS[i]) for i in pair]) for pair in ((8, 9), (10, 11), (12, 13), (14, 15))]
 
+TOK_SEMS = [sum(len(w[0]) - 1 for w in TOK_WAYS[:ch]) for ch in range(CHUNKS + 1)]
+HID_SEMS = [sum(len(w[0]) - 1 for w in HID_WAYS[:ch]) for ch in range(CHUNKS + 1)]
 SHIFTS = {
     (sign * (block[0] - after[0]) % NY, sign * (block[1] - after[1]) % NZ)
     for groups, _ in TOK_WAYS + HID_WAYS for group in groups for _, block, nexts in group for after in nexts for sign in (1, -1)
@@ -92,37 +94,38 @@
 LHS = (0, 1, 0, 1)
 
 ORDER = [
-    ("tok", 0, 0), ("tok", 1, 0), ("tok", 2, 0), ("tok", 0, 1), ("tok", 0, 2), ("tok", 0, 3),
-    ("tok", 0, 4), ("tok", 0, 5), ("tok", 1, 1), ("tok", 1, 2), ("tok", 1, 3), ("tok", 1, 4),
-    ("tok", 1, 5), ("tok", 2, 1), ("tok", 2, 2), ("tok", 2, 3), ("tok", 2, 4), ("tok", 0, 6),
-    ("tok", 0, 9), ("tok", 0, 7), ("tok", 0, 10), ("tok", 0, 8), ("tok", 1, 9), ("tok", 3, 0),
-    ("tok", 1, 6), ("tok", 1, 7), ("tok", 1, 10), ("tok", 1, 8), ("tok", 2, 5), ("tok", 2, 7),
-    ("tok", 2, 6), ("tok", 0, 15), ("tok", 2, 8), ("tok", 0, 11), ("tok", 0, 12), ("tok", 0, 13),
-    ("tok", 0, 14), ("pack", 0, 0), ("theirs", 0, 2), ("tok", 3, 1), ("tok", 3, 2), ("tok", 1, 12),
-    ("theirs", 0, 1), ("tok", 3, 4), ("theirs", 0, 3), ("tok", 3, 3), ("theirs", 0, 0), ("tok", 1, 11),
-    ("tok", 1, 15), ("mine", 0, 2), ("tok", 1, 13), ("tok", 1, 14), ("pack", 1, 0), ("theirs", 1, 2),
-    ("mine", 0, 1), ("tok", 2, 9), ("mine", 0, 3), ("tok", 2, 12), ("theirs", 1, 1), ("mine", 0, 0),
-    ("tok", 2, 10), ("theirs", 1, 3), ("tok", 2, 11), ("theirs", 1, 0), ("tok", 3, 5), ("mine", 1, 2),
-    ("tok", 3, 6), ("tok", 3, 9), ("mine", 1, 1), ("mine", 1, 3), ("tok", 3, 7), ("tok", 3, 8),
-    ("mine", 1, 0), ("tok", 2, 13), ("tok", 2, 14), ("pack", 2, 0), ("theirs", 2, 2), ("theirs", 2, 1),
-    ("theirs", 2, 3), ("theirs", 2, 0), ("act", 0, 0), ("mine", 2, 2), ("tok", 3, 10), ("tok", 3, 14),
-    ("tok", 3, 11), ("mine", 2, 1), ("tok", 3, 12), ("tok", 3, 13), ("pack", 3, 0), ("mine", 2, 3),
-    ("act", 1, 0), ("mine", 2, 0), ("theirs", 3, 2), ("theirs", 3, 1), ("theirs", 3, 3), ("hid", 0, 2),
-    ("theirs", 3, 0), ("hid", 0, 5), ("hid", 0, 1), ("hid", 0, 4), ("hid", 0, 3), ("mine", 3, 2),
-    ("mine", 3, 1), ("hid", 1, 2), ("hid", 1, 1), ("mine", 3, 3), ("act", 2, 0), ("mine", 3, 0),
-    ("hid", 1, 5), ("hid", 1, 3), ("hid", 1, 4), ("hid", 0, 7), ("hid", 0, 9), ("hid", 0, 10),
-    ("hid", 0, 6), ("hid", 0, 8), ("hid", 2, 2), ("hid", 2, 1), ("act", 3, 0), ("hid", 2, 3),
-    ("hid", 1, 7), ("hid", 1, 6), ("hid", 2, 4), ("hid", 1, 8), ("hid", 1, 9), ("hid", 0, 14),
-    ("hid", 0, 12), ("hid", 0, 15), ("hid", 0, 11), ("hid", 0, 13), ("hid", 3, 1), ("hid", 3, 2),
-    ("hid", 3, 4), ("hid", 3, 3), ("hid", 2, 7), ("hid", 2, 6), ("hid", 2, 5), ("hid", 1, 12),
-    ("hid", 1, 11), ("hid", 1, 10), ("hid", 1, 13), ("hid", 0, 17), ("hid", 0, 18), ("hid", 0, 16),
-    ("hid", 2, 8), ("mix", 0, 0), ("hid", 3, 6), ("hid", 3, 7), ("hid", 3, 5), ("hid", 3, 8),
-    ("hid", 2, 11), ("hid", 1, 17), ("hid", 1, 15), ("hid", 1, 14), ("hid", 1, 16), ("hid", 2, 9),
-    ("hid", 2, 10), ("hid", 2, 12), ("hid", 3, 12), ("finish", 0, 0), ("hid", 3, 10), ("hid", 3, 9),
-    ("hid", 1, 19), ("hid", 3, 11), ("hid", 1, 18), ("mix", 1, 0), ("hid", 2, 13), ("hid", 2, 15),
-    ("hid", 2, 16), ("hid", 2, 17), ("hid", 2, 14), ("mix", 2, 0), ("hid", 3, 15), ("hid", 3, 16),
-    ("hid", 3, 14), ("hid", 3, 17), ("hid", 3, 13), ("mix", 3, 0), ("finish", 1, 0), ("finish", 2, 0),
-    ("finish", 3, 0),
+    ("tok", 0, 0), ("tok", 2, 0), ("tok", 1, 0), ("tok", 0, 2), ("tok", 0, 1), ("tok", 0, 4),
+    ("tok", 0, 3), ("tok", 2, 1), ("tok", 2, 2), ("tok", 3, 0), ("tok", 2, 4), ("tok", 1, 2),
+    ("tok", 1, 1), ("tok", 2, 3), ("tok", 1, 4), ("tok", 1, 3), ("tok", 1, 5), ("tok", 0, 9),
+    ("tok", 0, 6), ("tok", 0, 8), ("tok", 0, 5), ("tok", 0, 7), ("tok", 3, 1), ("tok", 3, 2),
+    ("tok", 3, 5), ("tok", 3, 3), ("tok", 3, 4), ("tok", 2, 6), ("tok", 2, 5), ("tok", 2, 7),
+    ("tok", 2, 9), ("tok", 1, 7), ("tok", 2, 8), ("tok", 1, 8), ("tok", 1, 9), ("tok", 1, 10),
+    ("tok", 0, 13), ("tok", 1, 6), ("tok", 0, 11), ("tok", 0, 10), ("tok", 0, 14), ("tok", 0, 12),
+    ("pack", 0, 0), ("theirs", 0, 2), ("theirs", 0, 1), ("theirs", 0, 3), ("theirs", 0, 0), ("tok", 3, 7),
+    ("tok", 3, 6), ("tok", 3, 8), ("tok", 3, 9), ("tok", 2, 10), ("tok", 2, 11), ("tok", 3, 10),
+    ("mine", 0, 2), ("tok", 2, 12), ("tok", 2, 13), ("mine", 0, 1), ("tok", 1, 11), ("tok", 1, 12),
+    ("mine", 0, 3), ("tok", 1, 14), ("tok", 1, 15), ("tok", 1, 13), ("pack", 1, 0), ("theirs", 1, 2),
+    ("theirs", 1, 1), ("theirs", 1, 3), ("theirs", 1, 0), ("mine", 0, 0), ("tok", 3, 11), ("tok", 3, 12),
+    ("mine", 1, 2), ("tok", 3, 13), ("tok", 2, 14), ("mine", 1, 1), ("tok", 3, 14), ("mine", 1, 3),
+    ("tok", 2, 15), ("tok", 2, 16), ("tok", 3, 15), ("mine", 1, 0), ("pack", 3, 0), ("theirs", 3, 2),
+    ("act", 0, 0), ("theirs", 3, 1), ("theirs", 3, 3), ("theirs", 3, 0), ("mine", 3, 2), ("tok", 2, 17),
+    ("pack", 2, 0), ("theirs", 2, 2), ("theirs", 2, 1), ("theirs", 2, 3), ("theirs", 2, 0), ("mine", 3, 1),
+    ("mine", 3, 3), ("act", 1, 0), ("hid", 0, 2), ("hid", 0, 1), ("mine", 2, 2), ("hid", 0, 4),
+    ("hid", 0, 3), ("mine", 2, 1), ("mine", 2, 3), ("mine", 3, 0), ("hid", 0, 5), ("mine", 2, 0),
+    ("hid", 1, 3), ("hid", 1, 4), ("hid", 1, 1), ("hid", 1, 2), ("act", 3, 0), ("hid", 0, 10),
+    ("hid", 0, 9), ("hid", 0, 7), ("act", 2, 0), ("hid", 0, 8), ("hid", 1, 8), ("hid", 0, 6),
+    ("hid", 1, 7), ("hid", 1, 6), ("hid", 3, 3), ("hid", 1, 5), ("hid", 3, 2), ("hid", 3, 1),
+    ("hid", 3, 4), ("hid", 0, 13), ("hid", 0, 11), ("hid", 0, 12), ("hid", 2, 2), ("hid", 2, 1),
+    ("hid", 2, 5), ("hid", 2, 4), ("hid", 0, 15), ("hid", 2, 3), ("hid", 1, 10), ("hid", 1, 12),
+    ("hid", 0, 14), ("hid", 1, 9), ("hid", 3, 8), ("hid", 1, 11), ("hid", 3, 6), ("hid", 3, 5),
+    ("hid", 3, 7), ("hid", 2, 9), ("hid", 2, 7), ("hid", 0, 19), ("hid", 0, 17), ("hid", 2, 8),
+    ("hid", 0, 18), ("hid", 2, 6), ("hid", 0, 16), ("mix", 0, 0), ("hid", 1, 15), ("hid", 1, 13),
+    ("hid", 1, 16), ("hid", 1, 14), ("hid", 3, 12), ("hid", 3, 11), ("hid", 3, 10), ("hid", 3, 9),
+    ("hid", 2, 14), ("hid", 2, 11), ("hid", 2, 13), ("hid", 2, 10), ("hid", 2, 12), ("hid", 1, 20),
+    ("finish", 0, 0), ("hid", 1, 19), ("hid", 1, 17), ("hid", 1, 18), ("mix", 1, 0), ("hid", 3, 15),
+    ("hid", 3, 16), ("hid", 3, 13), ("hid", 3, 17), ("hid", 3, 14), ("mix", 3, 0), ("hid", 2, 17),
+    ("hid", 2, 15), ("hid", 2, 16), ("hid", 2, 18), ("mix", 2, 0), ("finish", 1, 0), ("finish", 3, 0),
+    ("finish", 2, 0),
 ]
 
 
@@ -155,13 +158,13 @@
             src_ref=src, dst_ref=dst, send_sem=sent, recv_sem=received, device_id=device, device_id_type=MESH
         )
 
-    tok_load = pltpu.make_async_copy(tok_hbm, tok, load_sem.at[0])
-    tok_load.start()
     barrier = pltpu.get_barrier_semaphore()
     peers = [at(dy=dy, dz=dz) for dy, dz in SHIFTS] + [at(dx=dx, dc=dc) for dx in range(NX) for dc in range(NC) if dx + dc]
     for peer in peers:
         pl.semaphore_signal(barrier, inc=1, device_id=peer, device_id_type=MESH)
 
+    tok_load = pltpu.make_async_copy(tok_hbm, tok, load_sem.at[0])
+    tok_load.start()
     w_wait = {}
     for i in (2, 1, 3, 0, 6, 5, 7, 4):
         share = at(dx=i % 4, dc=1 - i // 4)[0]
@@ -190,14 +193,14 @@
             copy.wait_send()
 
     class Gather:
-        def __init__(self, ref, ch, ways, cut, size, received, k):
-            self.ref, self.ch, self.size, self.received, self.k = ref, ch, size, received, k
+        def __init__(self, ref, ch, ways, cut, size, received, sems, k):
+            self.ref, self.ch, self.size, self.received, self.sems, self.k = ref, ch, size, received, sems[ch], k
             self.groups, self.trees = ways
             self.parts = ((0, cut), (cut, size - cut))
 
         def rows_of(self, count, g):
             rows = self.ref.at[self.ch, pl.ds(0, count)]
-            return remote(rows, rows, send_sem.at[self.k], self.received.at[self.ch, g], at(dy=1))
+            return remote(rows, rows, send_sem.at[self.k], self.received.at[self.sems + g], at(dy=1))
 
         def step(self, g):
             group = self.groups[g]
@@ -215,15 +218,15 @@
                     moves.append((-depth_of(self.trees[part], after), rows, at(dy=dy, dz=dz), self.arrives(part, after)))
             moves.sort(key=lambda move: move[0])
             for _, rows, device, there in moves:
-                remote(rows, rows, send_sem.at[self.k], self.received.at[self.ch, there - 1], device).start()
+                remote(rows, rows, send_sem.at[self.k], self.received.at[self.sems + there - 1], device).start()
 
         def arrives(self, part, block):
             for g, group in enumerate(self.groups):
                 if any(p == part and b == block for p, b, _ in group):
                     return g
 
-    tok_gather = [Gather(tok_all, ch, TOK_WAYS[ch], TOK_CUTS[ch], HALF, tok_recv, ch) for ch in range(CHUNKS)]
-    hid_gather = [Gather(hid_all, ch, HID_WAYS[ch], HID_CUTS[ch], ROWS, hid_recv, CHUNKS + ch) for ch in range(CHUNKS)]
+    tok_gather = [Gather(tok_all, ch, TOK_WAYS[ch], TOK_CUTS[ch], HALF, tok_recv, TOK_SEMS, ch) for ch in range(CHUNKS)]
+    hid_gather = [Gather(hid_all, ch, HID_WAYS[ch], HID_CUTS[ch], ROWS, hid_recv, HID_SEMS, CHUNKS + ch) for ch in range(CHUNKS)]
 
     def send_parts(ch, i):
         return remote(part_out.at[ch, i], part_in.at[ch, i], send_sem.at[2 * CHUNKS + ch], part_recv.at[ch, i], at(dc=1))
@@ -335,8 +338,8 @@
             pltpu.VMEM((CHUNKS, ROWS, 512), bf16),
             pltpu.VMEM((CHUNKS, 7 * 16, 512), bf16),
             pltpu.SemaphoreType.DMA((10,)),
-            pltpu.SemaphoreType.DMA((CHUNKS, max(len(w[0]) for w in TOK_WAYS) - 1)),
-            pltpu.SemaphoreType.DMA((CHUNKS, max(len(w[0]) for w in HID_WAYS) - 1)),
+            pltpu.SemaphoreType.DMA((TOK_SEMS[-1],)),
+            pltpu.SemaphoreType.DMA((HID_SEMS[-1],)),
             pltpu.SemaphoreType.DMA((CHUNKS, 4)),
             pltpu.SemaphoreType.DMA((CHUNKS,)),
             pltpu.SemaphoreType.DMA((CHUNKS,)),

time: 70.8 us -> 69.9 us (0.987)
  Pallas kernels: 70 us -> 69.2 us
    pallas_call x1, Pallas kernels: 70 us -> 69.2 us  [body(): pl.pallas_call(kernel, out_shape=pltpu.VMEM((64, 512), bf16), in_specs=[p...]
where the time goes in v4:
time: 69.9 us; the launch traced here: 69.8 us
  Pallas kernels  69.2 us (99%)
    pallas_call x1, Pallas kernels, body(): pl.pallas_call(kernel, out_shape=pltpu.VMEM((64, 512), bf16), in_specs=[p...  69.2 us

profile of v4, /device:TPU:1, one launch (start us, length us, event | category | flops | bytes accessed | tf_op | source)
XLA Modules:
  0.0 69.8 jit_solution(14142912906934219544)
XLA Ops:
  0.0 69.2 %shard_map.46 = bf16[64,512]{1,0:T(8,128)(2,1)S(1)} custom-call(bf16[64,512]{1,0:T(8,128)(2,1)} %bitcast.1, bf16[2048,1024]{1,0:T(8,128)(2,1)} %gate_hbm.1, bf16[2048,1024]{1,0:T(8,128)(2,1)} %up_hbm.1, bf16[32,128,512]{2,1,0:T(8,128)(2,1)} %down_hbm.1), custom_call_target="tpu_custom_call" | custom-call | flops 6442450944 | bytes 12582912 | tf_op jit(solution)/shard_map/pallas_call | solution.py:320
  69.2 0.6 copy.6
